TPU v7x, 32 devices: a whole 2x2x4 slice. The times are simulated.
32 devices in a mesh: fsdp: 16 (over z, y, core), ctx: 2 (over x).
Axes of the slice: x: 2, y: 2, z: 4, core: 2. Of those that a mesh axis runs over, the one named last changes fastest.
Arguments:
- hidden_in: bfloat16 [16, 1024, 1024], P('fsdp', 'ctx'), may hold values from -6 to 6
- positions: int32 [16, 1024], P('fsdp', 'ctx'), may hold values from 0 to 1023, as said below
- cotangent: bfloat16 [16, 1024, 1024], P('fsdp', 'ctx'), may hold values from -6 to 6
- norm_gain: float32 [1024], replicated, may hold values from 0.1 to 1.9
- w_query: bfloat16 [1024, 2048], P('fsdp'), may hold values from -0.1875 to 0.1875
- w_key: bfloat16 [1024, 1024], P('fsdp'), may hold values from -0.1875 to 0.1875
- w_value: bfloat16 [1024, 1024], P('fsdp'), may hold values from -0.1875 to 0.1875
- query_gain: float32 [128], replicated, may hold values from 0.1 to 1.9
- key_gain: float32 [128], replicated, may hold values from 0.1 to 1.9
- w_out: bfloat16 [2048, 1024], P('fsdp'), may hold values from -1 to 1
- mlp_gain: float32 [1024], replicated, may hold values from 0.1 to 1.9
- w_gate: bfloat16 [1024, 3072], P('fsdp'), may hold values from -0.1875 to 0.1875
- w_up: bfloat16 [1024, 3072], P('fsdp'), may hold values from -0.1875 to 0.1875
- w_down: bfloat16 [3072, 1024], P('fsdp'), may hold values from -0.109375 to 0.109375
Outputs:
- output: bfloat16 [16, 1024, 1024], P('fsdp', 'ctx')
- grad_input: bfloat16 [16, 1024, 1024], P('fsdp', 'ctx')
- grad_norm_gain: float32 [1024], replicated
- grad_w_query: float32 [1024, 2048], P('fsdp')
- grad_w_key: float32 [1024, 1024], P('fsdp')
- grad_w_value: float32 [1024, 1024], P('fsdp')
- grad_query_gain: float32 [128], replicated
- grad_key_gain: float32 [128], replicated
- grad_w_out: float32 [2048, 1024], P('fsdp')
- grad_mlp_gain: float32 [1024], replicated
- grad_w_gate: float32 [1024, 3072], P('fsdp')
- grad_w_up: float32 [1024, 3072], P('fsdp')
- grad_w_down: float32 [3072, 1024], P('fsdp')
Inputs may be any that keep to these rules, and one draw needn't show every extreme that they name: `positions`: positions start at 0 at each document's first token and rise by one within it. Documents in a sequence have 1024 // 10 to 1024 tokens, but a sequence may begin inside a document with fewer than 102 of its earlier tokens counted, and such a first piece may be shorter. Among the 1 sequence of each index of fsdp one holds a document that starts within its first 512 tokens and runs to its end.
All inputs are finite; a program needn't handle non-finite values.
Results may differ from a plain program's by a relative error of at most 0.02.
Values may be sent and summed in bfloat16 or wider, within the bound.
A program may use at most 256 MiB of HBM per device.

v0:
```python
import jax
import jax.numpy as jnp
from jax import lax
from jax.sharding import PartitionSpec as P

epsilon = 1e-06
theta_base = 1000000.0


def as_sent(shard):

    def short(part):
        return part.astype(jnp.bfloat16) if part.dtype == jnp.float32 else part

    return jax.tree.map(short, shard)


def norm_rows(values, gain_vec):
    inverse = lax.rsqrt(jnp.mean(values * values, axis=-1, keepdims=True) + epsilon)
    normed = values * inverse
    return (normed * gain_vec, normed, inverse)


def norm_back(grad_out, gain_vec, normed, inverse):
    scaled = grad_out * gain_vec
    grad_in = inverse * (scaled - normed * jnp.mean(scaled * normed, axis=-1, keepdims=True))
    return (grad_in, grad_out * normed)


def rope_tables(positions, head_dim):
    frequency = theta_base ** (-jnp.arange(0, head_dim, 2).astype(jnp.float32) / head_dim)
    angles = positions.astype(jnp.float32)[:, None] * frequency[None, :]
    angles = jnp.concatenate([angles, angles], axis=-1)
    return (jnp.cos(angles), jnp.sin(angles))


def rotate(values, cosine, sine_tab):
    half_dim = values.shape[-1] // 2
    turned = jnp.concatenate([-values[..., half_dim:], values[..., :half_dim]], axis=-1)
    return values * cosine[:, None, :] + turned * sine_tab[:, None, :]


def rotate_back(grad_out, cosine, sine_tab):
    half_dim = grad_out.shape[-1] // 2
    weighted = grad_out * sine_tab[:, None, :]
    turned = jnp.concatenate([weighted[..., half_dim:], -weighted[..., :half_dim]], axis=-1)
    return grad_out * cosine[:, None, :] + turned


def back_dot(grad_rows, weight):
    return lax.dot_general(
        grad_rows, weight, (((1,), (1,)), ((), ())), preferred_element_type=jnp.float32
    )


def weight_term(acts_in, grad_out):
    return lax.dot_general(
        acts_in, grad_out, (((0,), (0,)), ((), ())), preferred_element_type=jnp.float32
    )


def per_device(
    hidden_in,
    positions,
    cotangent,
    norm_gain,
    w_query,
    w_key,
    w_value,
    query_gain,
    key_gain,
    w_out,
    mlp_gain,
    w_gate,
    w_up,
    w_down,
):
    seqs_here, block_len, model_width = hidden_in.shape
    head_dim = query_gain.shape[0]
    kv_heads = w_key.shape[1] // head_dim
    q_heads = w_query.shape[1] // head_dim
    groups = q_heads // kv_heads
    ctx_count = lax.axis_size("ctx")
    ctx_rank = lax.axis_index("ctx")
    seq_total = block_len * ctx_count
    row_count = seqs_here * block_len
    scale_val = head_dim ** (-0.5)
    shards = (w_query, w_key, w_value, w_out, w_gate, w_up, w_down)
    full_weights = (
        lax.all_gather(shards[0], "fsdp", axis=0, tiled=True),
        lax.all_gather(shards[1], "fsdp", axis=0, tiled=True),
        lax.all_gather(shards[2], "fsdp", axis=0, tiled=True),
        lax.all_gather(shards[3], "fsdp", axis=0, tiled=True),
        lax.all_gather(shards[4], "fsdp", axis=0, tiled=True),
        lax.all_gather(shards[5], "fsdp", axis=0, tiled=True),
        lax.all_gather(shards[6], "fsdp", axis=0, tiled=True),
    )
    full_query, full_key, full_value, full_out, full_gate, full_up, full_down = full_weights
    residual = hidden_in.astype(jnp.float32).reshape(row_count, model_width)
    scaled_one, normed_one, inverse_one = norm_rows(residual, norm_gain)
    attn_in = scaled_one.astype(jnp.bfloat16)
    query_raw = jnp.dot(attn_in, full_query, preferred_element_type=jnp.float32).reshape(
        row_count, q_heads, head_dim
    )
    key_raw = jnp.dot(attn_in, full_key, preferred_element_type=jnp.float32).reshape(
        row_count, kv_heads, head_dim
    )
    value_bf = jnp.dot(attn_in, full_value, preferred_element_type=jnp.float32).astype(jnp.bfloat16)
    flat_pos = positions.reshape(row_count)
    cosine, sine_tab = rope_tables(flat_pos, head_dim)
    query_scaled, query_normed, query_inverse = norm_rows(query_raw, query_gain)
    query_bf = rotate(query_scaled, cosine, sine_tab).astype(jnp.bfloat16)
    key_scaled, key_normed, key_inverse = norm_rows(key_raw, key_gain)
    key_bf = rotate(key_scaled, cosine, sine_tab).astype(jnp.bfloat16)
    key_flat = key_bf.reshape(seqs_here, block_len, kv_heads * head_dim)
    value_flat = value_bf.reshape(seqs_here, block_len, kv_heads * head_dim)
    keys_all, values_all = (
        lax.all_gather(key_flat, "ctx", axis=1, tiled=True),
        lax.all_gather(value_flat, "ctx", axis=1, tiled=True),
    )
    query_five = query_bf.reshape(seqs_here, block_len, kv_heads, groups, head_dim)
    query_index = ctx_rank * block_len + jnp.arange(block_len, dtype=jnp.int32)
    doc_start = query_index[None, :] - positions

    def block_scores(key_source, block_idx):
        key_block = lax.dynamic_slice_in_dim(key_source, block_idx * block_len, block_len, 1)
        scores = (
            jnp.einsum(
                "sqkgd,spkd->skgqp", query_five, key_block, preferred_element_type=jnp.float32
            )
            * scale_val
        )
        key_index = block_idx * block_len + jnp.arange(block_len, dtype=jnp.int32)
        allowed = (key_index[None, None, :] <= query_index[None, :, None]) & (
            key_index[None, None, :] >= doc_start[:, :, None]
        )
        return (jnp.where(allowed[:, None, None, :, :], scores, -1e30), key_block)

    keys_four = keys_all.reshape(seqs_here, seq_total, kv_heads, head_dim)
    values_four = values_all.reshape(seqs_here, seq_total, kv_heads, head_dim)

    def stats_step(block_idx, carry_stats):
        running_max, running_sum = carry_stats
        scores, key_block = block_scores(keys_four, block_idx)
        new_max = jnp.maximum(running_max, jnp.max(scores, axis=-1))
        running_sum = running_sum * jnp.exp(running_max - new_max) + jnp.sum(
            jnp.exp(scores - new_max[..., None]), axis=-1
        )
        return (new_max, running_sum)

    stat_shape = (seqs_here, kv_heads, groups, block_len)
    row_max, row_sum = lax.fori_loop(
        0,
        ctx_rank + 1,
        stats_step,
        (jnp.full(stat_shape, -1e30, jnp.float32), jnp.zeros(stat_shape, jnp.float32)),
    )

    def output_step(block_idx, accum):
        scores, key_block = block_scores(keys_four, block_idx)
        probs_bf = (jnp.exp(scores - row_max[..., None]) / row_sum[..., None]).astype(jnp.bfloat16)
        value_block = lax.dynamic_slice_in_dim(values_four, block_idx * block_len, block_len, 1)
        return accum + jnp.einsum(
            "skgqp,spkd->sqkgd", probs_bf, value_block, preferred_element_type=jnp.float32
        )

    attn_f32 = lax.fori_loop(
        0,
        ctx_rank + 1,
        output_step,
        jnp.zeros((seqs_here, block_len, kv_heads, groups, head_dim), jnp.float32),
    )
    attn_bf = attn_f32.reshape(row_count, q_heads * head_dim).astype(jnp.bfloat16)
    middle = residual + jnp.dot(attn_bf, full_out, preferred_element_type=jnp.float32)
    scaled_two, normed_two, inverse_two = norm_rows(middle, mlp_gain)
    mlp_in = scaled_two.astype(jnp.bfloat16)
    gate_pre = jnp.dot(mlp_in, full_gate, preferred_element_type=jnp.float32)
    up_pre = jnp.dot(mlp_in, full_up, preferred_element_type=jnp.float32)
    sigmoid_gate = jax.nn.sigmoid(gate_pre)
    silu_gate = gate_pre * sigmoid_gate
    hidden_bf = (silu_gate * up_pre).astype(jnp.bfloat16)
    layer_out = middle + jnp.dot(hidden_bf, full_down, preferred_element_type=jnp.float32)
    output = layer_out.astype(jnp.bfloat16).reshape(seqs_here, block_len, model_width)
    back_weights = (
        lax.all_gather(shards[0], "fsdp", axis=0, tiled=True),
        lax.all_gather(shards[1], "fsdp", axis=0, tiled=True),
        lax.all_gather(shards[2], "fsdp", axis=0, tiled=True),
        lax.all_gather(shards[3], "fsdp", axis=0, tiled=True),
        lax.all_gather(shards[4], "fsdp", axis=0, tiled=True),
        lax.all_gather(shards[5], "fsdp", axis=0, tiled=True),
        lax.all_gather(shards[6], "fsdp", axis=0, tiled=True),
    )
    keys_back, values_back = (
        lax.all_gather(key_flat, "ctx", axis=1, tiled=True),
        lax.all_gather(value_flat, "ctx", axis=1, tiled=True),
    )
    back_query, back_key, back_value, back_out, back_gate, back_up, back_down = back_weights
    keys_again = keys_back.reshape(seqs_here, seq_total, kv_heads, head_dim)
    values_again = values_back.reshape(seqs_here, seq_total, kv_heads, head_dim)
    grad_rows = cotangent.reshape(row_count, model_width)
    down_grad = back_dot(grad_rows, back_down)
    grad_gate = (
        down_grad * up_pre * sigmoid_gate * (1.0 + gate_pre * (1.0 - sigmoid_gate))
    ).astype(jnp.bfloat16)
    grad_up = (down_grad * silu_gate).astype(jnp.bfloat16)
    grad_mlp_in = back_dot(grad_gate, back_gate) + back_dot(grad_up, back_up)
    grad_norm_two, mlp_gain_terms = norm_back(grad_mlp_in, mlp_gain, normed_two, inverse_two)
    grad_mid = grad_rows.astype(jnp.float32) + grad_norm_two
    grad_proj = grad_mid.astype(jnp.bfloat16)
    grad_attn = back_dot(grad_proj, back_out).astype(jnp.bfloat16)
    grad_five = grad_attn.reshape(seqs_here, block_len, kv_heads, groups, head_dim)
    delta = jnp.einsum("sqkgd,sqkgd->skgq", grad_five.astype(jnp.float32), attn_f32)

    def grad_step(block_idx, carry_grads):
        grad_query, grad_keys, grad_values = carry_grads
        scores, key_block = block_scores(keys_again, block_idx)
        probs = jnp.exp(scores - row_max[..., None]) / row_sum[..., None]
        value_block = lax.dynamic_slice_in_dim(values_again, block_idx * block_len, block_len, 1)
        grad_probs = jnp.einsum(
            "sqkgd,spkd->skgqp", grad_five, value_block, preferred_element_type=jnp.float32
        )
        grad_scores = (probs * (grad_probs - delta[..., None])).astype(jnp.bfloat16)
        grad_query = (
            grad_query
            + jnp.einsum(
                "skgqp,spkd->sqkgd", grad_scores, key_block, preferred_element_type=jnp.float32
            )
            * scale_val
        )
        key_part = (
            jnp.einsum(
                "skgqp,sqkgd->spkd", grad_scores, query_five, preferred_element_type=jnp.float32
            )
            * scale_val
        )
        value_part = jnp.einsum(
            "skgqp,sqkgd->spkd",
            probs.astype(jnp.bfloat16),
            grad_five,
            preferred_element_type=jnp.float32,
        )
        grad_keys = lax.dynamic_update_slice_in_dim(grad_keys, key_part, block_idx * block_len, 1)
        grad_values = lax.dynamic_update_slice_in_dim(
            grad_values, value_part, block_idx * block_len, 1
        )
        return (grad_query, grad_keys, grad_values)

    whole_shape = (seqs_here, seq_total, kv_heads, head_dim)
    grad_query, grad_keys, grad_values = lax.fori_loop(
        0,
        ctx_rank + 1,
        grad_step,
        (
            jnp.zeros((seqs_here, block_len, kv_heads, groups, head_dim), jnp.float32),
            jnp.zeros(whole_shape, jnp.float32),
            jnp.zeros(whole_shape, jnp.float32),
        ),
    )
    key_grad_own, value_grad_own = (
        lax.psum_scatter(
            grad_keys.reshape(seqs_here, seq_total, kv_heads * head_dim).astype(jnp.bfloat16),
            "ctx",
            scatter_dimension=1,
            tiled=True,
        ).astype(jnp.float32),
        lax.psum_scatter(
            grad_values.reshape(seqs_here, seq_total, kv_heads * head_dim).astype(jnp.bfloat16),
            "ctx",
            scatter_dimension=1,
            tiled=True,
        ).astype(jnp.float32),
    )
    key_unrot = rotate_back(key_grad_own.reshape(row_count, kv_heads, head_dim), cosine, sine_tab)
    key_raw_grad, key_gain_terms = norm_back(key_unrot, key_gain, key_normed, key_inverse)
    key_raw_bf = key_raw_grad.reshape(row_count, kv_heads * head_dim).astype(jnp.bfloat16)
    query_unrot = rotate_back(grad_query.reshape(row_count, q_heads, head_dim), cosine, sine_tab)
    query_raw_grad, query_gain_terms = norm_back(
        query_unrot, query_gain, query_normed, query_inverse
    )
    query_raw_bf = query_raw_grad.reshape(row_count, q_heads * head_dim).astype(jnp.bfloat16)
    value_raw_bf = value_grad_own.reshape(row_count, kv_heads * head_dim).astype(jnp.bfloat16)
    grad_attn_in = (
        back_dot(query_raw_bf, back_query)
        + back_dot(key_raw_bf, back_key)
        + back_dot(value_raw_bf, back_value)
    )
    grad_norm_one, norm_gain_terms = norm_back(grad_attn_in, norm_gain, normed_one, inverse_one)
    grad_input = (
        (grad_mid + grad_norm_one).astype(jnp.bfloat16).reshape(seqs_here, block_len, model_width)
    )
    gain_one, gain_query, gain_key, gain_two = lax.psum(
        (
            jnp.sum(norm_gain_terms, axis=0),
            jnp.sum(query_gain_terms, axis=(0, 1)),
            jnp.sum(key_gain_terms, axis=(0, 1)),
            jnp.sum(mlp_gain_terms, axis=0),
        ),
        ("fsdp", "ctx"),
    )
    weight_pairs = (
        (attn_in, query_raw_bf),
        (attn_in, key_raw_bf),
        (attn_in, value_raw_bf),
        (attn_bf, grad_proj),
        (mlp_in, grad_gate),
        (mlp_in, grad_up),
        (hidden_bf, grad_rows),
    )
    pieces = tuple(
        (
            lax.psum_scatter(
                weight_term(acts_in, grad_out).astype(jnp.bfloat16),
                "fsdp",
                scatter_dimension=0,
                tiled=True,
            ).astype(jnp.float32)
            for acts_in, grad_out in weight_pairs
        )
    )
    weight_grads = jax.tree.map(
        lambda part: part.astype(jnp.float32), lax.psum(as_sent(pieces), "ctx")
    )
    grad_wq, grad_wk, grad_wv, grad_wo, grad_wg, grad_wu, grad_wd = weight_grads
    return (
        output,
        grad_input,
        gain_one,
        grad_wq,
        grad_wk,
        grad_wv,
        gain_query,
        gain_key,
        grad_wo,
        gain_two,
        grad_wg,
        grad_wu,
        grad_wd,
    )


def solution(mesh):
    in_specs = (
        P("fsdp", "ctx", None),
        P("fsdp", "ctx"),
        P("fsdp", "ctx", None),
        P(),
        P("fsdp", None),
        P("fsdp", None),
        P("fsdp", None),
        P(),
        P(),
        P("fsdp", None),
        P(),
        P("fsdp", None),
        P("fsdp", None),
        P("fsdp", None),
    )
    out_specs = (
        P("fsdp", "ctx", None),
        P("fsdp", "ctx", None),
        P(),
        P("fsdp", None),
        P("fsdp", None),
        P("fsdp", None),
        P(),
        P(),
        P("fsdp", None),
        P(),
        P("fsdp", None),
        P("fsdp", None),
        P("fsdp", None),
    )
    return jax.shard_map(
        per_device, mesh=mesh, in_specs=in_specs, out_specs=out_specs, check_vma=False
    )
```

profile of v0, /device:TPU:0, one launch (start us, length us, event | category | flops | bytes accessed | tf_op | source)
XLA Modules:
  0.0 1310.8 jit_solution(275446278528645502)
XLA Ops:
  10.3 44.0 %all-gather.11.cloned.1.call-done = bf16[1024,1024]{1,0:T(8,128)(2,1)} async-done(((bf16[64,1024]{1,0:T(8,128)(2,1)}), bf16[1024,1024]{1,0:T(8,128)(2,1)}) %all-gather.11.cloned.1.call-update) | async-done | bytes 2097168 | tf_op jit(solution)/shard_map/all_gather | solution.py:92
  54.3 4.2 convolution_convert_fusion.8
  59.7 37.0 %all-gather.13.cloned.1.call-done = bf16[1024,1024]{1,0:T(8,128)(2,1)} async-done(((bf16[64,1024]{1,0:T(8,128)(2,1)}), bf16[1024,1024]{1,0:T(8,128)(2,1)}) %all-gather.13.cloned.1.call-update) | async-done | bytes 2097168 | tf_op jit(solution)/shard_map/all_gather | solution.py:91
  96.7 4.0 copy.41
  100.7 3.0 multiply_reduce_fusion.8
  110.7 20.0 %all-gather.27.cloned.1.call-done = bf16[1024,1024]{1,0:T(8,128)(2,1)} async-done(((bf16[512,1024]{1,0:T(8,128)(2,1)}), bf16[1024,1024]{1,0:T(8,128)(2,1)}) %all-gather.27.cloned.1.call-update) | async-done | bytes 2097168 | tf_op jit(solution)/shard_map/all_gather | solution.py:119
  130.7 3.5 copy.90
  134.2 31.6 %all-gather.15.cloned.1.call-done = bf16[1,1024,1024]{1,2,0:T(8,128)(2,1)} async-done(((bf16[1,512,1024]{1,2,0:T(8,128)(2,1)}), bf16[1,1024,1024]{1,2,0:T(8,128)(2,1)}) %all-gather.15.cloned.1.call-update) | async-done | bytes 2097168 | tf_op jit(solution)/shard_map/all_gather | solution.py:118
  165.8 3.9 copy.46
  169.8 48.7 %all-gather.17.cloned.1.call-done = bf16[1024,2048]{1,0:T(8,128)(2,1)} async-done(((bf16[64,2048]{1,0:T(8,128)(2,1)}), bf16[1024,2048]{1,0:T(8,128)(2,1)}) %all-gather.17.cloned.1.call-update) | async-done | bytes 4194320 | tf_op jit(solution)/shard_map/all_gather | solution.py:90
  218.4 6.4 copy.42
  224.9 4.8 multiply_reduce_fusion.2
  232.4 2.8 fusion.69
  235.1 3.0 copy.47
  238.2 18.4 %while.39 = (s32[]{:T(128)}, f32[1,8,2,512]{3,2,1,0:T(2,128)S(1)}, f32[1,8,2,512]{3,2,1,0:T(2,128)S(1)}, s32[]{:T(128)}, s32[1,512]{1,0:T(1,128)S(1)}, /*index=5...) while((s32[]{:T(128)}, f32[1,8,2,512]{3,2,1,0:T(2,128)S(1)}, ...), condition=%wide.region_6.7_spmd.clone, body=%wide.region_3.6_spmd.clone.sunk | while | flops 1103905792 | bytes 37923000 | solution.py:152
  238.5 8.7 fusion.173
  247.3 9.3 exponential_reduce_fusion.2
  259.1 12.3 while.40
  262.4 9.0 bitcast_add_fusion.7
  271.4 4.6 convert_element_type.199
  276.0 5.5 multiply_reduce_fusion.7
  281.8 50.6 %all-gather.21.cloned.1.call-done = bf16[1024,3072]{1,0:T(8,128)(2,1)} async-done(((bf16[64,3072]{1,0:T(8,128)(2,1)}), bf16[1024,3072]{1,0:T(8,128)(2,1)}) %all-gather.21.cloned.1.call-update) | async-done | bytes 6291472 | tf_op jit(solution)/shard_map/all_gather | solution.py:94
  332.4 8.1 fusion.121
  340.4 54.7 %all-gather.23.cloned.1.call-done = bf16[1024,3072]{1,0:T(8,128)(2,1)} async-done(((bf16[64,3072]{1,0:T(8,128)(2,1)}), bf16[1024,3072]{1,0:T(8,128)(2,1)}) %all-gather.23.cloned.1.call-update) | async-done | bytes 6291472 | tf_op jit(solution)/shard_map/all_gather | solution.py:95
  395.1 8.1 fusion.122
  403.3 54.6 %all-gather.25.cloned.1.call-done = bf16[3072,1024]{1,0:T(8,128)(2,1)} async-done(((bf16[192,1024]{1,0:T(8,128)(2,1)}), bf16[3072,1024]{1,0:T(8,128)(2,1)}) %all-gather.25.cloned.1.call-update) | async-done | bytes 6291472 | tf_op jit(solution)/shard_map/all_gather | solution.py:96
  457.9 11.9 multiply_convert_fusion
  469.8 8.5 fusion.123
  478.3 4.5 multiply_reduce_fusion.3
  490.9 2.7 reshape.647
  495.9 3.4 bitcast_convert_fusion
  499.3 7.6 copy.69
  506.9 4.6 fusion.70
  517.3 50.8 %while.41 = (s32[]{:T(128)}, f32[1,512,8,2,128]{1,4,3,2,0:T(8,128)}, bf16[1,1024,8,128]{1,3,2,0:T(8,128)(2,1)}, bf16[1,1024,8,128]{1,3,2,0:T(8,128)(2,1)}, s32[]...) while((s32[]{:T(128)}, ...), condition=%wide.region_12.13_spmd.clone, body=%wide.region_11.12_spmd.clone.sunk | while | flops 5406196736 | bytes 117025032 | solution.py:249
  517.6 9.8 fusion.187
  527.4 9.3 fusion.188
  536.7 8.4 bitcast_add_fusion.8
  545.1 9.1 fusion.189
  555.7 7.3 fusion.190
  565.2 2.8 constant_dynamic-update-slice_fusion.3
  569.0 2.9 bitcast_multiply_fusion.1
  574.1 4.1 multiply_reduce_fusion
  581.0 4.7 convolution_convert_fusion.4
  587.2 5.9 convolution_convert_fusion.3
  593.2 56.2 %reduce-scatter.10.cloned.1.call-done = bf16[1,512,1024]{1,2,0:T(8,128)(2,1)} async-done(((bf16[1,1024,1024]{1,2,0:T(8,128)(2,1)}), bf16[1,512,1024]{1,2,0:T(8,128)(2,1)}) %reduce-scatter.10.cloned.1.call-update) | async-done | bytes 1048592 | tf_op jit(solution)/shard_map/reduce_scatter | solution.py:260
  655.4 2.9 convolution_convert_fusion.7
  658.3 25.3 %reduce-scatter.12.cloned.1.call-done = bf16[1,512,1024]{1,2,0:T(8,128)(2,1)} async-done(((bf16[1,1024,1024]{1,2,0:T(8,128)(2,1)}), bf16[1,512,1024]{1,2,0:T(8,128)(2,1)}) %reduce-scatter.12.cloned.1.call-update) | async-done | bytes 1048592 | tf_op jit(solution)/shard_map/reduce_scatter | solution.py:266
  683.6 4.0 convolution_convert_fusion.6
  687.9 8.4 convolution_convert_fusion.2
  696.3 8.6 convolution_convert_fusion.1
  705.0 8.5 convolution_convert_fusion
  713.8 9.2 fusion.91
  723.0 36.6 %reduce-scatter.14.cloned.1.call-done = bf16[64,2048]{1,0:T(8,128)(2,1)} async-done(((bf16[1024,2048]{1,0:T(8,128)(2,1)}), bf16[64,2048]{1,0:T(8,128)(2,1)}) %reduce-scatter.14.cloned.1.call-update) | async-done | bytes 262160 | tf_op jit(solution)/shard_map/reduce_scatter | solution.py:311
  759.7 75.8 %reduce-scatter.20.cloned.1.call-done = bf16[128,1024]{1,0:T(8,128)(2,1)} async-done(((bf16[2048,1024]{1,0:T(8,128)(2,1)}), bf16[128,1024]{1,0:T(8,128)(2,1)}) %reduce-scatter.20.cloned.1.call-update) | async-done | bytes 262160 | tf_op jit(solution)/shard_map/reduce_scatter | solution.py:311
  835.5 64.3 %reduce-scatter.16.cloned.1.call-done = bf16[64,1024]{1,0:T(8,128)(2,1)} async-done(((bf16[1024,1024]{1,0:T(8,128)(2,1)}), bf16[64,1024]{1,0:T(8,128)(2,1)}) %reduce-scatter.16.cloned.1.call-update) | async-done | bytes 131088 | tf_op jit(solution)/shard_map/reduce_scatter | solution.py:311
  899.8 64.6 %reduce-scatter.18.cloned.1.call-done = bf16[64,1024]{1,0:T(8,128)(2,1)} async-done(((bf16[1024,1024]{1,0:T(8,128)(2,1)}), bf16[64,1024]{1,0:T(8,128)(2,1)}) %reduce-scatter.18.cloned.1.call-update) | async-done | bytes 131088 | tf_op jit(solution)/shard_map/reduce_scatter | solution.py:311
  964.5 88.0 %reduce-scatter.22.cloned.1.call-done = bf16[64,3072]{1,0:T(8,128)(2,1)} async-done(((bf16[1024,3072]{1,0:T(8,128)(2,1)}), bf16[64,3072]{1,0:T(8,128)(2,1)}) %reduce-scatter.22.cloned.1.call-update) | async-done | bytes 393232 | tf_op jit(solution)/shard_map/reduce_scatter | solution.py:311
  1052.5 88.7 %reduce-scatter.24.cloned.1.call-done = bf16[64,3072]{1,0:T(8,128)(2,1)} async-done(((bf16[1024,3072]{1,0:T(8,128)(2,1)}), bf16[64,3072]{1,0:T(8,128)(2,1)}) %reduce-scatter.24.cloned.1.call-update) | async-done | bytes 393232 | tf_op jit(solution)/shard_map/reduce_scatter | solution.py:311
  1141.2 88.3 %reduce-scatter.26.cloned.1.call-done = bf16[192,1024]{1,0:T(8,128)(2,1)} async-done(((bf16[3072,1024]{1,0:T(8,128)(2,1)}), bf16[192,1024]{1,0:T(8,128)(2,1)}) %reduce-scatter.26.cloned.1.call-update) | async-done | bytes 393232 | tf_op jit(solution)/shard_map/reduce_scatter | solution.py:311
  1229.5 3.4 fusion.95
  1235.8 4.2 fusion.84
  1240.0 40.2 %all-reduce = (f32[1024]{0:T(1024)}, f32[128]{0:T(128)}, f32[128]{0:T(128)}, f32[1024]{0:T(1024)}) all-reduce(f32[1024]{0:T(1024)S(1)} %get-tuple-element.337, f32[128]{0:T(128)S(1)} %get-tuple-element.331, f32[128]{0:T(128)S(1)} %get-tuple-element.333, f32[1024]{0:T(1024)S(1)} %copy-done.43), channel_id=1, replica_groups=mesh['fsdp'=16,'ctx'=2] {'fsdp','ctx'}, use_global_device_ids=true, to_apply=%region_19.20 | all-reduce | flops 2304 | bytes 18432 | tf_op jit(solution)/shard_map/psum | solution.py:291
  1280.2 3.1 fusion.92
  1283.4 10.6 all-reduce.4.cloned.1.call-done
  (195 shorter events, 66.8 us)
Async XLA Ops:
  7.2 47.1 %all-gather.11.cloned.1.call-start = ((), (), s32[]{:S(2)}) async-start(), calls=%async_computation.9 | async-start | bytes 2228224 | tf_op jit(solution)/shard_map/all_gather | solution.py:92
  7.9 88.8 %all-gather.13.cloned.1.call-start = ((), (), s32[]{:S(2)}) async-start(), calls=%async_computation.10 | async-start | bytes 2228224 | tf_op jit(solution)/shard_map/all_gather | solution.py:91
  8.7 122.0 %all-gather.27.cloned.1.call-start = ((), (), s32[]{:S(2)}) async-start(), calls=%async_computation.26 | async-start | bytes 3145728 | tf_op jit(solution)/shard_map/all_gather | solution.py:119
  10.2 214.6 %copy-start.35 = (f32[512]{0:T(512)}, f32[512]{0:T(512)S(1)}, u32[]{:S(2)}) copy-start(f32[512]{0:T(512)S(1)} %add_rsqrt_fusion.3) | copy-start | bytes 6148
  10.3 48.3 %copy-start.44 = (s32[1,512]{1,0:T(1,128)S(1)}, s32[1,512]{1,0:T(1,128)}, u32[]{:S(2)}) copy-start(s32[1,512]{1,0:T(1,128)} %param.21) | copy-start | bytes 6148
  58.5 107.3 %all-gather.15.cloned.1.call-start = ((), (), s32[]{:S(2)}) async-start(), calls=%async_computation.11 | async-start | bytes 3145728 | tf_op jit(solution)/shard_map/all_gather | solution.py:118
  59.7 171.6 %copy-start.6 = (f32[512,128]{0,1:T(8,128)}, f32[512,128]{0,1:T(8,128)S(1)}, u32[]{:S(2)}) copy-start(f32[512,128]{0,1:T(8,128)S(1)} %get-tuple-element.434) | copy-start | bytes 786436
  59.7 171.6 %copy-start.13 = (f32[512,128]{0,1:T(8,128)}, f32[512,128]{0,1:T(8,128)S(1)}, u32[]{:S(2)}) copy-start(f32[512,128]{0,1:T(8,128)S(1)} %get-tuple-element.435) | copy-start | bytes 786436
  96.7 4.0 copy-start.16
  96.7 4.0 copy-start.41
  100.7 3.0 copy-start.37
  106.7 111.7 %all-gather.17.cloned.1.call-start = ((), (), s32[]{:S(2)}) async-start(), calls=%async_computation.12 | async-start | bytes 4456448 | tf_op jit(solution)/shard_map/all_gather | solution.py:90
  107.3 168.6 %all-gather.19.cloned.1.call-start = ((), (), s32[]{:S(2)}) async-start(), calls=%async_computation.13 | async-start | bytes 4456448 | tf_op jit(solution)/shard_map/all_gather | solution.py:93
  107.9 224.4 %all-gather.21.cloned.1.call-start = ((), (), s32[]{:S(2)}) async-start(), calls=%async_computation.14 | async-start | bytes 6684672 | tf_op jit(solution)/shard_map/all_gather | solution.py:94
  108.7 286.5 %all-gather.23.cloned.1.call-start = ((), (), s32[]{:S(2)}) async-start(), calls=%async_computation.15 | async-start | bytes 6684672 | tf_op jit(solution)/shard_map/all_gather | solution.py:95
  109.4 348.5 %all-gather.25.cloned.1.call-start = ((), (), s32[]{:S(2)}) async-start(), calls=%async_computation.16 | async-start | bytes 6684672 | tf_op jit(solution)/shard_map/all_gather | solution.py:96
  110.1 539.3 %reduce-scatter.10.cloned.1.call-start = ((), (), s32[]{:S(2)}) async-start(), calls=%async_computation.17 | async-start | bytes 3145728 | tf_op jit(solution)/shard_map/reduce_scatter | solution.py:260
  224.8 4.9 copy-start.39
  229.7 2.7 copy-start.2
  229.7 2.7 copy-start.27
  271.4 4.6 copy-start
  271.4 4.6 copy-start.17
  276.0 5.5 copy-start.34
  281.5 201.3 %copy-start.12 = (f32[512,1024]{1,0:T(8,128)}, f32[512,1024]{1,0:T(8,128)S(1)}, u32[]{:S(2)}) copy-start(f32[512,1024]{1,0:T(8,128)S(1)} %get-tuple-element.443) | copy-start | bytes 6291460
  281.8 113.4 %copy-start.23 = (bf16[512,1024]{1,0:T(8,128)(2,1)}, bf16[512,1024]{1,0:T(8,128)(2,1)S(1)}, u32[]{:S(2)}) copy-start(bf16[512,1024]{1,0:T(8,128)(2,1)S(1)} %multiply_convert_fusion.5) | copy-start | bytes 3145732
  469.8 8.5 copy-start.48
  469.8 8.5 copy-start.47
  469.8 8.5 copy-start.45
  478.3 4.5 copy-start.24
  482.8 2.9 copy-start.46
  483.4 1.4 copy-start.10
  493.6 2.3 copy-start.9
  517.6 9.8 copy-start.1
  568.1 115.5 %reduce-scatter.12.cloned.1.call-start = ((), (), s32[]{:S(2)}) async-start(), calls=%async_computation.18 | async-start | bytes 3145728 | tf_op jit(solution)/shard_map/reduce_scatter | solution.py:266
  568.8 190.9 %reduce-scatter.14.cloned.1.call-start = ((), (), s32[]{:S(2)}) async-start(), calls=%async_computation.19 | async-start | bytes 4456448 | tf_op jit(solution)/shard_map/reduce_scatter | solution.py:311
  571.9 2.2 copy-start.3
  571.9 2.2 copy-start.7
  571.9 2.2 copy-start.28
  571.9 2.2 copy-start.40
  578.2 2.8 copy-start.18
  578.2 2.8 copy-start.36
  578.2 2.8 copy-start.42
  579.6 1.4 copy-start.21
  585.7 1.6 copy-start.11
  585.7 249.8 %reduce-scatter.20.cloned.1.call-start = ((), (), s32[]{:S(2)}) async-start(), calls=%async_computation.22 | async-start | bytes 4456448 | tf_op jit(solution)/shard_map/reduce_scatter | solution.py:311
  593.2 306.6 %reduce-scatter.16.cloned.1.call-start = ((), (), s32[]{:S(2)}) async-start(), calls=%async_computation.20 | async-start | bytes 2228224 | tf_op jit(solution)/shard_map/reduce_scatter | solution.py:311
  650.9 1.6 copy-start.5
  650.9 1.8 copy-start.8
  650.9 1.8 copy-start.30
  651.0 1.8 copy-start.38
  653.6 1.8 copy-start.19
  658.2 306.2 %reduce-scatter.18.cloned.1.call-start = ((), (), s32[]{:S(2)}) async-start(), calls=%async_computation.21 | async-start | bytes 2228224 | tf_op jit(solution)/shard_map/reduce_scatter | solution.py:311
  687.6 364.8 %reduce-scatter.22.cloned.1.call-start = ((), (), s32[]{:S(2)}) async-start(), calls=%async_computation.23 | async-start | bytes 6684672 | tf_op jit(solution)/shard_map/reduce_scatter | solution.py:311
  696.3 444.9 %reduce-scatter.24.cloned.1.call-start = ((), (), s32[]{:S(2)}) async-start(), calls=%async_computation.24 | async-start | bytes 6684672 | tf_op jit(solution)/shard_map/reduce_scatter | solution.py:311
  705.0 524.5 %reduce-scatter.26.cloned.1.call-start = ((), (), s32[]{:S(2)}) async-start(), calls=%async_computation.25 | async-start | bytes 6684672 | tf_op jit(solution)/shard_map/reduce_scatter | solution.py:311
  713.5 580.5 %all-reduce.4.cloned.1.call-start = ((), (), s32[]{:S(2)}) async-start(), calls=%async_computation.27 | async-start | bytes 3932160 | tf_op jit(solution)/shard_map/psum | solution.py:321
  1229.5 3.4 copy-start.20
  1229.5 3.4 copy-start.26
  1232.9 2.2 copy-start.15
  1232.9 2.9 copy-start.22
  1235.8 4.2 copy-start.43
  1294.0 7.0 copy-start.33
  1294.0 7.9 copy-start.32
  1295.9 7.0 copy-start.31
  (4 other events, 4.6 us)
Sparse Core Ops, SparseCore 0:
  10.2 44.0 all-gather.10
  56.5 40.1 all-gather.12
  98.8 31.8 all-gather.26
  132.7 33.1 all-gather.14
  167.8 50.5 all-gather.16
  220.5 49.1 all-gather.18
  272.0 60.3 all-gather.20
  334.6 60.4 all-gather.22
  397.4 60.4 all-gather.24
  568.2 81.1 reduce-scatter.9
  651.7 31.8 reduce-scatter.11
  687.3 72.3 reduce-scatter.13
  764.0 71.4 reduce-scatter.19
  839.1 60.6 reduce-scatter.15
  903.9 60.5 reduce-scatter.17
  968.2 84.1 reduce-scatter.21
  1056.8 84.3 reduce-scatter.23
  1145.0 84.4 reduce-scatter.25
  1232.4 61.5 all-reduce.3
where the time goes:
time: 1320 us; the launch traced here: 1310 us
  waiting for transfers between devices  945 us (72%)
  matrix products  184 us (14%)
  local copies, waits for them, and re-layouts  66.9 us (5%)
  other arithmetic  57.9 us (4%)
  blocking collectives  40.2 us (3%)
  between operations  15.1 us (1%)
    reduce_scatter x7, waiting for transfers between devices, per_device(): lax.psum_scatter(weight_term(acts_in, grad_out).astype(jnp.bfloat16), 'fs...  506 us
    reduce_scatter x1, waiting for transfers between devices, per_device(): lax.psum_scatter(grad_keys.reshape(seqs_here, seq_total, kv_heads * head_...  56.2 us
    all_gather x1, waiting for transfers between devices, per_device(): lax.all_gather(shards[5], 'fsdp', axis=0, tiled=True)  54.7 us
    all_gather x1, waiting for transfers between devices, per_device(): lax.all_gather(shards[6], 'fsdp', axis=0, tiled=True)  54.6 us
    all_gather x1, waiting for transfers between devices, per_device(): lax.all_gather(shards[4], 'fsdp', axis=0, tiled=True)  50.6 us
    all_gather x1, waiting for transfers between devices, per_device(): lax.all_gather(shards[0], 'fsdp', axis=0, tiled=True)  48.7 us
    all_gather x1, waiting for transfers between devices, per_device(): lax.all_gather(shards[2], 'fsdp', axis=0, tiled=True)  44 us
    dot_general x7, matrix products, weight_term(): lax.dot_general(acts_in, grad_out, (((0,), (0,)), ((), ())), preferred_el...  42.9 us
  transfers between devices with their start and end apart: 19, of which 18 were waited for; matrix products, arithmetic and copies ran while one was open for 14% of the time, Pallas kernels for 0%

commit v1 on v0

--- a/solution.py
+++ b/solution.py
@@ -1,7 +1,13 @@
+import functools
+
 import jax
 import jax.numpy as jnp
 from jax import lax
+from jax.experimental import pallas as pl
+from jax.experimental.pallas import tpu as pltpu
 from jax.sharding import PartitionSpec as P
+
+MESH = pl.DeviceIdType.MESH
 
 epsilon = 1e-06
 theta_base = 1000000.0
@@ -59,7 +65,416 @@
     )
 
 
+def place():
+    f = lax.axis_index("fsdp")
+    return f // 4, (f // 2) % 2, f % 2, lax.axis_index("ctx")
+
+
+def enter(z, y, c, x):
+    bar = pltpu.get_barrier_semaphore()
+
+    def hail(z2, y2, c2, x2):
+        pl.semaphore_signal(bar, inc=1, device_id=(z2 * 4 + y2 * 2 + c2, x2), device_id_type=MESH)
+
+    hail(z, y, c, 1 - x)
+    hail(z, 1 - y, c, x)
+    hail(z, y, 1 - c, x)
+
+    @pl.when(z > 0)
+    def _():
+        hail(z - 1, y, c, x)
+
+    @pl.when(z < 3)
+    def _():
+        hail(z + 1, y, c, x)
+
+    pl.semaphore_wait(bar, 4 + (z * (3 - z)) // 2)
+
+
+class Gather:
+    def __init__(self, index, own, full, sems, at):
+        self.g, self.own, self.full = index, own, full
+        self.zr, self.yr, self.xr, self.cr, self.zs, self.ys, self.xs, self.cs, self.ls = sems
+        self.z, self.y, self.c, self.x = at
+        self.rows, self.cols = own.shape
+        unit = self.cols // 8
+        x = self.x
+        self.ywin = pl.ds(pl.multiple_of(x * 3 * unit, 128), 5 * unit)
+        self.xwin = pl.ds(pl.multiple_of(x * 5 * unit, 128), 3 * unit)
+        self.xgot = pl.ds(pl.multiple_of((1 - x) * 5 * unit, 128), 3 * unit)
+        self.all = pl.ds(0, self.cols)
+        self.ends = []
+
+    def part(self, z2, y2, c2, win):
+        f2 = z2 * 4 + y2 * 2 + c2
+        return self.full.at[pl.ds(pl.multiple_of(f2 * self.rows, 16), self.rows), win]
+
+    def send(self, src, dst, ssem, rsem, to):
+        z2, y2, c2, x2 = to
+        return pltpu.make_async_remote_copy(
+            src_ref=src, dst_ref=dst, send_sem=ssem, recv_sem=rsem,
+            device_id=(z2 * 4 + y2 * 2 + c2, x2), device_id_type=MESH)
+
+    def z_copy(self, zs, up, first):
+        dst = self.part(zs, self.y, self.c, self.ywin)
+        src = self.own.at[:, self.ywin] if first else dst
+        z2 = self.z + 1 if up else self.z - 1
+        return self.send(src, dst, self.zs.at[self.g, zs, 1 if up else 0], self.zr.at[self.g, zs], (z2, self.y, self.c, self.x))
+
+    def y_copy(self, zs, first):
+        dst = self.part(zs, self.y, self.c, self.ywin)
+        src = self.own.at[:, self.ywin] if first else dst
+        return self.send(src, dst, self.ys.at[self.g, zs], self.yr.at[self.g, zs], (self.z, 1 - self.y, self.c, self.x))
+
+    def x_copy(self, zs, y2):
+        dst = self.part(zs, y2, self.c, self.xwin)
+        s = zs * 2 + y2
+        return self.send(dst, dst, self.xs.at[self.g, s], self.xr.at[self.g, s], (self.z, self.y, self.c, 1 - self.x))
+
+    def c_copy(self, zs, y2, win, piece, first=False):
+        dst = self.part(zs, y2, self.c, win)
+        src = self.own if first else dst
+        s = (zs * 2 + y2) * 2 + piece
+        return self.send(src, dst, self.cs.at[self.g, s], self.cr.at[self.g, s], (self.z, self.y, 1 - self.c, self.x))
+
+    def await_(self, dst, sem):
+        pltpu.make_async_copy(dst, dst, sem).wait()
+
+    def local(self):
+        return pltpu.make_async_copy(self.own, self.part(self.z, self.y, self.c, self.all), self.ls.at[self.g])
+
+    def begin(self):
+        z = self.z
+
+        @pl.when(z < 3)
+        def _():
+            self.z_copy(z, True, True).start()
+
+        @pl.when(z > 0)
+        def _():
+            self.z_copy(z, False, True).start()
+
+        self.y_copy(z, True).start()
+        self.c_copy(z, self.y, self.all, 0, True).start()
+        self.local().start()
+
+    def spread(self, zs, up):
+        self.await_(self.part(zs, self.y, self.c, self.ywin), self.zr.at[self.g, zs])
+
+        @pl.when(self.z < 3 if up else self.z > 0)
+        def _():
+            self.z_copy(zs, up, False).start()
+
+        self.y_copy(zs, False).start()
+        self.x_copy(zs, self.y).start()
+        self.c_copy(zs, self.y, self.ywin, 0).start()
+
+    def along_z(self, k):
+        @pl.when(self.z >= k)
+        def _():
+            self.spread(self.z - k, True)
+
+        @pl.when(self.z + k <= 3)
+        def _():
+            self.spread(self.z + k, False)
+
+    def over_y(self, zs):
+        self.await_(self.part(zs, 1 - self.y, self.c, self.ywin), self.yr.at[self.g, zs])
+        self.x_copy(zs, 1 - self.y).start()
+        self.c_copy(zs, 1 - self.y, self.ywin, 0).start()
+
+    def along_y(self, k):
+        if k == 0:
+            self.over_y(self.z)
+            return
+
+        @pl.when(self.z >= k)
+        def _():
+            self.over_y(self.z - k)
+
+        @pl.when(self.z + k <= 3)
+        def _():
+            self.over_y(self.z + k)
+
+    def over_x(self, zs, y2):
+        self.await_(self.part(zs, y2, self.c, self.xgot), self.xr.at[self.g, zs * 2 + y2])
+        self.c_copy(zs, y2, self.xgot, 1).start()
+
+    def along_x(self, k):
+        if k == 0:
+            self.over_x(self.z, 1 - self.y)
+            return
+
+        for y2 in (self.y, 1 - self.y):
+            @pl.when(self.z >= k)
+            def _():
+                self.over_x(self.z - k, y2)
+
+            @pl.when(self.z + k <= 3)
+            def _():
+                self.over_x(self.z + k, y2)
+
+    def finish(self):
+        z, y = self.z, self.y
+        self.local().wait()
+        c = 1 - self.c
+        self.await_(self.part(z, y, c, self.all), self.cr.at[self.g, (z * 2 + y) * 2])
+        for k in range(0, 4):
+            for y2 in ((y, 1 - y) if k else (1 - y,)):
+                for zs, ok in ((z - k, z >= k), (z + k, z + k <= 3))[: 2 if k else 1]:
+                    @pl.when(ok)
+                    def _():
+                        s = (zs * 2 + y2) * 2
+                        self.await_(self.part(zs, y2, c, self.ywin), self.cr.at[self.g, s])
+                        self.await_(self.part(zs, y2, c, self.xgot), self.cr.at[self.g, s + 1])
+
+    def drain(self):
+        z, y = self.z, self.y
+
+        @pl.when(z < 3)
+        def _():
+            self.z_copy(z, True, True).wait_send()
+
+        @pl.when(z > 0)
+        def _():
+            self.z_copy(z, False, True).wait_send()
+
+        self.y_copy(z, True).wait_send()
+        self.c_copy(z, y, self.all, 0, True).wait_send()
+        self.x_copy(z, 1 - y).wait_send()
+        self.c_copy(z, 1 - y, self.ywin, 0).wait_send()
+        self.c_copy(z, 1 - y, self.xgot, 1).wait_send()
+        for k in range(1, 4):
+            for zs, ok, more, up in ((z - k, z >= k, z < 3, True), (z + k, z + k <= 3, z > 0, False)):
+                @pl.when(ok)
+                def _():
+                    @pl.when(more)
+                    def _():
+                        self.z_copy(zs, up, False).wait_send()
+
+                    self.y_copy(zs, False).wait_send()
+                    for y2 in (y, 1 - y):
+                        self.x_copy(zs, y2).wait_send()
+                        self.c_copy(zs, y2, self.ywin, 0).wait_send()
+                        self.c_copy(zs, y2, self.xgot, 1).wait_send()
+
+
+def gather_sems(n):
+    return [pltpu.SemaphoreType.DMA(s) for s in ((n, 4), (n, 4), (n, 8), (n, 16), (n, 4, 2), (n, 4), (n, 8), (n, 16), (n,))]
+
+
+def gather_kernel(n, *refs):
+    owns, fulls, sems = refs[:n], refs[n:2 * n], refs[2 * n:]
+    at = place()
+    enter(*at)
+    gs = [Gather(i, owns[i], fulls[i], sems, at) for i in range(n)]
+    plan = []
+    steps = ["begin", ("along_z", 1), ("along_z", 2), ("along_z", 3), ("along_y", 0), ("along_y", 1), ("along_y", 2), ("along_y", 3),
+             ("along_x", 0), ("along_x", 1), ("along_x", 2), ("along_x", 3)]
+    lag = 4
+    slots = {}
+    for i in range(n):
+        for j, s in enumerate(steps):
+            slots.setdefault(i * lag + j, []).append((i, s))
+    for t in sorted(slots):
+        for i, s in sorted(slots[t], key=lambda e: e[0]):
+            if isinstance(s, str):
+                getattr(gs[i], s)()
+            else:
+                getattr(gs[i], s[0])(s[1])
+    for g in gs:
+        g.finish()
+    for g in gs:
+        g.drain()
+
+
+def gather_all(shards):
+    n = len(shards)
+    return pl.pallas_call(
+        functools.partial(gather_kernel, n),
+        out_shape=[jax.ShapeDtypeStruct((s.shape[0] * 16, s.shape[1]), s.dtype) for s in shards],
+        in_specs=[pl.BlockSpec(memory_space=pl.ANY)] * n,
+        out_specs=[pl.BlockSpec(memory_space=pl.ANY)] * n,
+        scratch_shapes=gather_sems(n),
+        compiler_params=pltpu.CompilerParams(collective_id=1, has_side_effects=True),
+        name="gather_weights",
+    )(*shards)
+
+
+class Reduce:
+    def __init__(self, index, part, out, bufs, sems, at):
+        self.g, self.p, self.out = index, part, out
+        self.a, self.cb, self.xb, self.yb, self.zb, self.fb = bufs
+        self.sc, self.sx, self.sy, self.sz, self.sf, self.ls = sems
+        self.z, self.y, self.c, self.x = at
+        self.rows, self.cols = part.shape[-2:]
+        u = self.u = self.cols // 8
+        x = self.x
+        self.ywin = pl.ds(pl.multiple_of(x * 2 * u, 128), 6 * u)
+        self.xsend = pl.ds(pl.multiple_of((1 - x) * 6 * u, 128), 2 * u)
+        self.xgot = pl.ds(pl.multiple_of(x * 6 * u, 128), 2 * u)
+
+    def send(self, src, dst, sem, to):
+        z2, y2, c2, x2 = to
+        return pltpu.make_async_remote_copy(
+            src_ref=src, dst_ref=dst, send_sem=sem[0], recv_sem=sem[1],
+            device_id=(z2 * 4 + y2 * 2 + c2, x2), device_id_type=MESH)
+
+    def c_copy(self):
+        return self.send(self.p.at[:, :, 1 - self.c], self.cb, (self.sc.at[self.g, 0], self.sc.at[self.g, 1]), (self.z, self.y, 1 - self.c, self.x))
+
+    def load(self):
+        return pltpu.make_async_copy(self.p.at[:, :, self.c], self.a, self.ls.at[self.g])
+
+    def x_copy(self):
+        return self.send(self.a.at[:, :, :, self.xsend], self.xb, (self.sx.at[self.g, 0], self.sx.at[self.g, 1]), (self.z, self.y, self.c, 1 - self.x))
+
+    def y_copy(self):
+        return self.send(self.a.at[:, 1 - self.y, :, self.ywin], self.yb, (self.sy.at[self.g, 0], self.sy.at[self.g, 1]), (self.z, 1 - self.y, self.c, self.x))
+
+    def z_copy(self, zs, up):
+        z2 = self.z + 1 if up else self.z - 1
+        slot = zs if up else jnp.where(zs == z2, 4, zs)
+        return self.send(self.a.at[zs, self.y, :, self.ywin], self.zb.at[slot], (self.sz.at[self.g, 0, zs], self.sz.at[self.g, 1, slot]), (z2, self.y, self.c, self.x))
+
+    def f_copy(self):
+        return self.send(self.a.at[self.z, self.y, :, self.ywin], self.fb, (self.sf.at[self.g, 0], self.sf.at[self.g, 1]), (self.z, self.y, self.c, 1 - self.x))
+
+    def add(self, dst, win, src):
+        step = 16
+
+        @pl.loop(0, self.rows, step=step)
+        def _(r):
+            rr = pl.ds(pl.multiple_of(r, step), step)
+            dst[rr, win] = dst[rr, win] + src[rr, :]
+
+    def add_all(self, zs_, ys_, win, src):
+        @pl.loop(0, 4)
+        def _(zz):
+            for yy in ys_:
+                self.add(self.a.at[zz, yy], win, src(zz, yy))
+
+    def go(self):
+        self.c_copy().start()
+        self.load().start()
+
+    def s_c(self):
+        self.load().wait()
+        self.c_copy().wait_recv()
+        self.add_all(4, (0, 1), pl.ds(0, self.cols), lambda zz, yy: self.cb.at[zz, yy])
+        self.x_copy().start()
+
+    def s_x(self):
+        self.x_copy().wait_recv()
+        self.add_all(4, (0, 1), self.xgot, lambda zz, yy: self.xb.at[zz, yy])
+        self.y_copy().start()
+
+    def s_y(self):
+        self.y_copy().wait_recv()
+        self.add_all(4, (self.y,), self.ywin, lambda zz, yy: self.yb.at[zz])
+
+    def await_(self, dst, sem):
+        pltpu.make_async_copy(dst, dst, sem).wait()
+
+    def take(self, zs, slot):
+        self.await_(self.zb.at[slot], self.sz.at[self.g, 1, slot])
+        self.add(self.a.at[zs, self.y], self.ywin, self.zb.at[slot])
+
+    def s_z(self, k):
+        z = self.z
+        up = 4 - k
+        for zs, ok, first, d in ((up, up > z, z == 0, True), (3 - up, 3 - up < z, z == 3, False)):
+            @pl.when(ok)
+            def _():
+                @pl.when(jnp.logical_not(first))
+                def _():
+                    self.take(zs, zs)
+
+                self.z_copy(zs, d).start()
+
+    def s_own(self):
+        @pl.when(self.z > 0)
+        def _():
+            self.take(self.z, self.z)
+
+        @pl.when(self.z < 3)
+        def _():
+            self.take(self.z, 4)
+
+        self.f_copy().start()
+
+    def s_f(self):
+        u = self.u
+        self.f_copy().wait_recv()
+        mine = self.a.at[self.z, self.y]
+        f32 = jnp.float32
+        for xx, solo, both_f, got, got_f in ((0, 0, 0, 6, 4), (1, 6, 2, 0, 0)):
+            @pl.when(self.x == xx)
+            def _():
+                @pl.loop(0, self.rows, step=16)
+                def _(r):
+                    rr = pl.ds(pl.multiple_of(r, 16), 16)
+                    self.out[rr, solo * u:(solo + 2) * u] = mine[rr, solo * u:(solo + 2) * u].astype(f32)
+                    self.out[rr, 2 * u:6 * u] = mine[rr, 2 * u:6 * u].astype(f32) + self.fb[rr, both_f * u:(both_f + 4) * u].astype(f32)
+                    self.out[rr, got * u:(got + 2) * u] = self.fb[rr, got_f * u:(got_f + 2) * u].astype(f32)
+
+    def drain(self):
+        self.c_copy().wait_send()
+        self.x_copy().wait_send()
+        self.y_copy().wait_send()
+        self.f_copy().wait_send()
+        for k in (1, 2, 3):
+            up = 4 - k
+            for zs, ok, d in ((up, up > self.z, True), (3 - up, 3 - up < self.z, False)):
+                @pl.when(ok)
+                def _():
+                    self.z_copy(zs, d).wait_send()
+
+
+def reduce_bufs(shape):
+    r, c = shape
+    u = c // 8
+    return [pltpu.VMEM(s, jnp.bfloat16) for s in ((4, 2, r, c), (4, 2, r, c), (4, 2, r, 2 * u), (4, r, 6 * u), (5, r, 6 * u), (r, 6 * u))]
+
+
+def reduce_sems(n):
+    return [pltpu.SemaphoreType.DMA(s) for s in ((n, 2), (n, 2), (n, 2), (n, 2, 5), (n, 2), (n,))]
+
+
+def reduce_kernel(n, lag, *refs):
+    parts, outs, bufs, sems = refs[:n], refs[n:2 * n], refs[2 * n:2 * n + 6 * n], refs[8 * n:]
+    at = place()
+    enter(*at)
+    rs = [Reduce(i, parts[i], outs[i], bufs[6 * i:6 * i + 6], sems, at) for i in range(n)]
+    steps = [("go",), ("s_c",), ("s_x",), ("s_y",), ("s_z", 1), ("s_z", 2), ("s_z", 3), ("s_own",), ("s_f",)]
+    slots = {}
+    for i in range(n):
+        for j, s in enumerate(steps):
+            slots.setdefault(i * lag + j, []).append((i, s))
+    for t in sorted(slots):
+        for i, s in sorted(slots[t], key=lambda e: e[0]):
+            getattr(rs[i], s[0])(*s[1:])
+    for r in rs:
+        r.drain()
+
+
+def reduce_all(parts, lag=1):
+    n = len(parts)
+    parts = [p.reshape(4, 2, 2, p.shape[0] // 16, p.shape[1]) for p in parts]
+    return pl.pallas_call(
+        functools.partial(reduce_kernel, n, lag),
+        out_shape=[jax.ShapeDtypeStruct(p.shape[-2:], jnp.float32) for p in parts],
+        in_specs=[pl.BlockSpec(memory_space=pl.ANY)] * n,
+        out_specs=[pl.BlockSpec(memory_space=pltpu.VMEM)] * n,
+        scratch_shapes=[b for p in parts for b in reduce_bufs(p.shape[-2:])] + reduce_sems(n),
+        compiler_params=pltpu.CompilerParams(collective_id=2, has_side_effects=True, vmem_limit_bytes=60 * 2**20),
+        name="reduce_grads",
+    )(*parts)
+
+
 def per_device(
+    gather_weights,
+    reduce_grads,
     hidden_in,
     positions,
     cotangent,
@@ -86,15 +501,7 @@
     row_count = seqs_here * block_len
     scale_val = head_dim ** (-0.5)
     shards = (w_query, w_key, w_value, w_out, w_gate, w_up, w_down)
-    full_weights = (
-        lax.all_gather(shards[0], "fsdp", axis=0, tiled=True),
-        lax.all_gather(shards[1], "fsdp", axis=0, tiled=True),
-        lax.all_gather(shards[2], "fsdp", axis=0, tiled=True),
-        lax.all_gather(shards[3], "fsdp", axis=0, tiled=True),
-        lax.all_gather(shards[4], "fsdp", axis=0, tiled=True),
-        lax.all_gather(shards[5], "fsdp", axis=0, tiled=True),
-        lax.all_gather(shards[6], "fsdp", axis=0, tiled=True),
-    )
+    full_weights = gather_weights(shards)
     full_query, full_key, full_value, full_out, full_gate, full_up, full_down = full_weights
     residual = hidden_in.astype(jnp.float32).reshape(row_count, model_width)
     scaled_one, normed_one, inverse_one = norm_rows(residual, norm_gain)
@@ -181,15 +588,7 @@
     hidden_bf = (silu_gate * up_pre).astype(jnp.bfloat16)
     layer_out = middle + jnp.dot(hidden_bf, full_down, preferred_element_type=jnp.float32)
     output = layer_out.astype(jnp.bfloat16).reshape(seqs_here, block_len, model_width)
-    back_weights = (
-        lax.all_gather(shards[0], "fsdp", axis=0, tiled=True),
-        lax.all_gather(shards[1], "fsdp", axis=0, tiled=True),
-        lax.all_gather(shards[2], "fsdp", axis=0, tiled=True),
-        lax.all_gather(shards[3], "fsdp", axis=0, tiled=True),
-        lax.all_gather(shards[4], "fsdp", axis=0, tiled=True),
-        lax.all_gather(shards[5], "fsdp", axis=0, tiled=True),
-        lax.all_gather(shards[6], "fsdp", axis=0, tiled=True),
-    )
+    back_weights = full_weights
     keys_back, values_back = (
         lax.all_gather(key_flat, "ctx", axis=1, tiled=True),
         lax.all_gather(value_flat, "ctx", axis=1, tiled=True),
@@ -306,20 +705,10 @@
         (mlp_in, grad_up),
         (hidden_bf, grad_rows),
     )
-    pieces = tuple(
-        (
-            lax.psum_scatter(
-                weight_term(acts_in, grad_out).astype(jnp.bfloat16),
-                "fsdp",
-                scatter_dimension=0,
-                tiled=True,
-            ).astype(jnp.float32)
-            for acts_in, grad_out in weight_pairs
-        )
-    )
-    weight_grads = jax.tree.map(
-        lambda part: part.astype(jnp.float32), lax.psum(as_sent(pieces), "ctx")
-    )
+    partials = tuple(
+        weight_term(acts_in, grad_out).astype(jnp.bfloat16) for acts_in, grad_out in weight_pairs
+    )
+    weight_grads = reduce_grads(partials)
     grad_wq, grad_wk, grad_wv, grad_wo, grad_wg, grad_wu, grad_wd = weight_grads
     return (
         output,
@@ -338,6 +727,40 @@
     )
 
 
+def gather_plain(shards):
+    return tuple(lax.all_gather(shard, "fsdp", axis=0, tiled=True) for shard in shards)
+
+
+def reduce_plain(partials):
+    pieces = tuple(
+        lax.psum_scatter(part, "fsdp", scatter_dimension=0, tiled=True) for part in partials
+    )
+    return tuple(part.astype(jnp.float32) for part in lax.psum(pieces, "ctx"))
+
+
+def gather_grid(shards):
+    order = (1, 2, 0, 3, 4, 5, 6)
+    full = gather_all([shards[i] for i in order])
+    return tuple(full[order.index(i)] for i in range(7))
+
+
+def reduce_grid(partials):
+    order = (6, 5, 4, 3, 0, 1, 2)
+    done = reduce_all([partials[i] for i in order])
+    return tuple(done[order.index(i)] for i in range(7))
+
+
+def is_grid(mesh):
+    if dict(mesh.shape) != {"fsdp": 16, "ctx": 2}:
+        return False
+    for f in range(16):
+        for x in range(2):
+            device = mesh.devices[f, x]
+            if tuple(device.coords) != (x, (f // 2) % 2, f // 4) or device.core_on_chip != f % 2:
+                return False
+    return True
+
+
 def solution(mesh):
     in_specs = (
         P("fsdp", "ctx", None),
@@ -370,6 +793,7 @@
         P("fsdp", None),
         P("fsdp", None),
     )
+    plan = (gather_grid, reduce_grid) if is_grid(mesh) else (gather_plain, reduce_plain)
     return jax.shard_map(
-        per_device, mesh=mesh, in_specs=in_specs, out_specs=out_specs, check_vma=False
-    )
+        functools.partial(per_device, *plan), mesh=mesh, in_specs=in_specs, out_specs=out_specs, check_vma=False
+    )

time: 1320 us -> 820 us (0.62)
  waiting for transfers between devices: 945 us -> 122 us
  Pallas kernels: 0 us -> 347 us
  matrix products: 184 us -> 157 us
    reduce_scatter x7 -> x0, waiting for transfers between devices: 506 us -> none  [per_device(): lax.psum_scatter(weight_term(acts_in, grad_out).astype(jnp.bfloat16), 'fs...]
    pallas_call x0 -> x2, Pallas kernels: none -> 347 us  [the longest x1 208 us: reduce_all(): pl.pallas_call(functools.partial(reduce_kernel, n, lag), out_shape=[jax.S...]
    all_gather x7 -> x0, waiting for transfers between devices: 290 us -> none  [the longest x1 54.7 us: per_device(): lax.all_gather(shards[5], 'fsdp', axis=0, tiled=True)]
    all_gather x1, waiting for transfers between devices: 20 us -> 0.02 us  [per_device(): lax.all_gather(value_flat, 'ctx', axis=1, tiled=True)]
    unnamed x101 -> x140, local copies, waits for them, and re-layouts: 33.3 us -> 40.4 us
  transfers between devices with their start and end apart: 19 -> 4, of which waited for: 18 -> 3; matrix products, arithmetic and copies ran while one was open for 14% -> 10% of each run, Pallas kernels for 0% -> 0%
where the time goes in v1:
time: 820 us; the launch traced here: 811 us
  Pallas kernels  347 us (42%)
  matrix products  157 us (19%)
  waiting for transfers between devices  122 us (15%)
  local copies, waits for them, and re-layouts  73.8 us (9%)
  other arithmetic  51.4 us (6%)
  blocking collectives  43.9 us (5%)
  between operations  15.1 us (2%)
    pallas_call x1, Pallas kernels, reduce_all(): pl.pallas_call(functools.partial(reduce_kernel, n, lag), out_shape=[jax.S...  208 us
    pallas_call x1, Pallas kernels, gather_all(): pl.pallas_call(functools.partial(gather_kernel, n), out_shape=[jax.ShapeD...  138 us
    reduce_scatter x1, waiting for transfers between devices, per_device(): lax.psum_scatter(grad_keys.reshape(seqs_here, seq_total, kv_heads * head_...  66.7 us
    psum x1, blocking collectives, per_device(): lax.psum((jnp.sum(norm_gain_terms, axis=0), jnp.sum(query_gain_terms, axi...  43.9 us
    unnamed x140, local copies, waits for them, and re-layouts  40.4 us
    dot_general x7, matrix products, back_dot(): lax.dot_general(grad_rows, weight, (((1,), (1,)), ((), ())), preferred_el...  35 us
    all_gather x1, waiting for transfers between devices, per_device(): lax.all_gather(key_flat, 'ctx', axis=1, tiled=True)  31.7 us
    dot_general x7, matrix products, weight_term(): lax.dot_general(acts_in, grad_out, (((0,), (0,)), ((), ())), preferred_el...  31.5 us
  transfers between devices with their start and end apart: 4, of which 3 were waited for; matrix products, arithmetic and copies ran while one was open for 10% of the time, Pallas kernels for 0%

profile of v1, /device:TPU:0, one launch (start us, length us, event | category | flops | bytes accessed | tf_op | source)
XLA Modules:
  0.0 810.8 jit_solution(11011465136517415125)
XLA Ops:
  8.8 138.1 %gather_weights.1 = (bf16[1024,1024]{1,0:T(8,128)(2,1)}, bf16[1024,1024]{1,0:T(8,128)(2,1)}, bf16[1024,2048]{1,0:T(8,128)(2,1)}, bf16[2048,1024]{1,0:T(8,128)(2,...) custom-call(bf16[64,1024]{1,0:T(8,128)(2,1)} %refs_0_.1, ...), custom_call_target="tpu_custom_call" | custom-call | tf_op jit(solution)/shard_map/gather_weights/pallas_call | solution.py:293
  147.0 3.9 convolution_convert_fusion.8
  150.9 3.9 copy.73
  156.0 3.3 multiply_reduce_fusion.8
  160.7 1.7 fusion.94
  162.9 6.4 copy.74
  169.3 4.7 multiply_reduce_fusion.2
  176.7 2.7 fusion.73
  179.4 3.0 copy.48
  182.4 3.6 copy.95
  186.0 31.7 %all-gather.4.cloned.1.call-done = bf16[1,1024,1024]{1,2,0:T(8,128)(2,1)} async-done(((bf16[1,512,1024]{1,2,0:T(8,128)(2,1)}), bf16[1,1024,1024]{1,2,0:T(8,128)(2,1)}) %all-gather.4.cloned.1.call-update) | async-done | bytes 2097168 | tf_op jit(solution)/shard_map/all_gather | solution.py:525
  217.7 3.9 copy.47
  221.6 18.1 %while.39 = (s32[]{:T(128)}, f32[1,8,2,512]{3,2,1,0:T(2,128)S(1)}, f32[1,8,2,512]{3,2,1,0:T(2,128)S(1)}, s32[]{:T(128)}, s32[1,512]{1,0:T(1,128)S(1)}, /*index=5...) while((s32[]{:T(128)}, f32[1,8,2,512]{3,2,1,0:T(2,128)S(1)}, ...), condition=%wide.region_6.7_spmd.clone, body=%wide.region_3.6_spmd.clone.sunk | while | flops 1103905792 | bytes 37923000 | solution.py:559
  221.9 8.5 %fusion.177 = (f32[8,2,512]{2,1,0:T(2,128)S(1)}, f32[8,512,512,2]{2,1,3,0:T(8,128)}) fusion(pred[512,512]{0,1:T(8,128)(4,1)S(1)} %compare_and_fusion.6, bf16[1,512,8,2,128]{4,1,3,2,0:T(8,128)(2,1)S(1)} %get-tuple-element.711, bf16[1,1024,8,128]{3,1,2,0:T(8,128)(2,1)} %get-tuple-element.710, s32[]{:T(128)S(6)} %select_n.65), kind=kOutput, calls=%fused_computation.5.clone.1 | convolution fusion | flops 1086316544 | bytes 20217860 | tf_op jit(solution)/shard_map/while/body/sqkgd,spkd->skgqp/dot_general | solution.py:535
  230.5 9.2 %exponential_reduce_fusion.2 = f32[8,2,512]{2,1,0:T(2,128)S(1)} fusion(f32[8,512,512,2]{2,1,3,0:T(8,128)} %get-tuple-element.652, f32[8,2,512]{2,1,0:T(2,128)S(1)} %bitcast.392, pred[512,512]{0,1:T(8,128)(4,1)S(1)} %compare_and_fusion.6), kind=kLoop, calls=%fused_computation.4.clone.1 | loop fusion | flops 16769024 | bytes 17104896 | tf_op jit(solution)/shard_map/while/body/reduce_sum | solution.py:553
  239.8 2.5 broadcast.381.clone
  242.2 12.2 %while.40 = (s32[]{:T(128)}, f32[1,512,8,2,128]{1,4,3,2,0:T(8,128)}, s32[]{:T(128)}, bf16[1,1024,8,128]{3,2,1,0:T(8,128)(2,1)}, s32[1,512]{1,0:T(1,128)S(1)}, /*...) while((s32[]{:T(128)}, ...), condition=%wide.region_8.9_spmd.clone, body=%wide.region_7.8_spmd.clone.sunk | while | flops 2170291200 | bytes 17377484 | solution.py:574
  245.4 9.0 %bitcast_add_fusion.7 = f32[1,512,8,2,128]{1,4,3,2,0:T(8,128)} fusion(f32[1,512,8,2,128]{1,4,3,2,0:T(8,128)} %get-tuple-element.732, f32[8,2,512]{2,1,0:T(2,128)S(1)} %bitcast.419, f32[8,2,512]{2,1,0:T(2,128)S(1)} %bitcast.407, pred[512,512]{0,1:T(8,128)(4,1)S(1)} %compare_and_fusion.7, bf16[1,512,8,2,128]{4,1,3,2,0:T(8,128)(2,1)S(1)} %get-tuple-element.751, ...), kind=kOutput, calls=%fused_computation.23.clone.1 | convolution fusion | flops 2169503744 | bytes 12910596 | tf_op jit(solution)/shard_map/while/body/skgqp,spkd->sqkgd/dot_general | solution.py:570
  254.5 3.3 convert_element_type.164
  257.8 1.8 copy-done.49
  259.6 2.5 multiply_reduce_fusion.7
  262.4 5.4 fusion.125
  267.9 5.4 fusion.126
  273.3 10.4 %fusion.70 = (bf16[512,3072]{1,0:T(8,128)(2,1)S(1)}, bf16[512,3072]{1,0:T(8,128)(2,1)}, bf16[512,3072]{1,0:T(8,128)(2,1)}) fusion(f32[512,3072]{1,0:T(8,128)} %fusion.125, f32[512,3072]{1,0:T(8,128)} %fusion.126, bf16[3072,1024]{1,0:T(8,128)(2,1)S(1)} %bitcast.430, bf16[1,512,1024]{2,1,0:T(8,128)(2,1)S(1)} %copy-done.28), kind=kOutput, calls=%fused_computation.75 | convolution fusion | flops 3244818432 | bytes 29360128 | tf_op jit(solution)/shard_map/dot_general | solution.py:57
  283.7 7.6 fusion.127
  291.3 4.4 multiply_reduce_fusion.3
  298.6 2.4 convolution_convert_fusion.5
  301.0 2.7 reshape.667
  303.7 2.7 reshape.668
  306.5 2.3 copy.53
  308.8 3.4 bitcast_convert_fusion
  312.2 7.6 copy.72
  319.8 4.6 fusion.74
  324.4 2.5 broadcast.381
  330.1 50.8 %while.41 = (s32[]{:T(128)}, f32[1,512,8,2,128]{1,4,3,2,0:T(8,128)}, bf16[1,1024,8,128]{1,3,2,0:T(8,128)(2,1)}, bf16[1,1024,8,128]{1,3,2,0:T(8,128)(2,1)}, s32[]...) while((s32[]{:T(128)}, ...), condition=%wide.region_12.13_spmd.clone, body=%wide.region_11.12_spmd.clone.sunk | while | flops 5406196736 | bytes 117025032 | solution.py:648
  330.4 9.8 %fusion.191 = f32[1,8,2,512,512]{3,4,2,1,0:T(8,128)} fusion(f32[8,2,512]{2,1,0:T(2,128)S(1)} %bitcast.420, f32[8,2,512]{2,1,0:T(2,128)S(1)} %bitcast.408, pred[512,512]{0,1:T(8,128)(4,1)S(1)} %compare_and_fusion.8, bf16[1,512,8,2,128]{4,1,3,2,0:T(8,128)(2,1)} %get-tuple-element.802, bf16[1,1024,8,128]{3,1,2,0:T(8,128)(2,1)} %get-tuple-element.800, ...), kind=kOutput, calls=%fused_computation.41.clone.1 | convolution fusion | flops 1090519040 | bytes 20250628 | tf_op jit(solution)/shard_map/while/body/sqkgd,spkd->skgqp/dot_general | solution.py:535
  340.2 9.3 %fusion.192 = bf16[1,8,2,512,512]{3,4,2,1,0:T(8,128)(2,1)} fusion(f32[1,8,2,512,512]{3,4,2,1,0:T(8,128)} %fusion.191, f32[8,2,512]{2,1,0:T(2,128)S(1)} %bitcast.422, bf16[1,512,8,2,128]{4,1,3,2,0:T(8,128)(2,1)S(1)} %get-tuple-element.806, bf16[1,512,8,128]{3,2,1,0:T(8,128)(2,1)S(1)} %constant_dynamic-slice_fusion.5), kind=kOutput, calls=%fused_computation.37.clone.1 | convolution fusion | flops 1086324736 | bytes 28344320 | tf_op jit(solution)/shard_map/while/body/sqkgd,spkd->skgqp/dot_general | solution.py:618
  349.5 8.4 %bitcast_add_fusion.8 = f32[1,512,8,2,128]{1,4,3,2,0:T(8,128)} fusion(f32[1,512,8,2,128]{1,4,3,2,0:T(8,128)} %get-tuple-element.778, bf16[1,8,2,512,512]{3,4,2,1,0:T(8,128)(2,1)} %fusion.192, bf16[1,1024,8,128]{3,1,2,0:T(8,128)(2,1)} %get-tuple-element.800, s32[]{:T(128)S(6)} %select_n.69), kind=kOutput, calls=%fused_computation.49.clone.1 | convolution fusion | flops 1075838976 | bytes 17825796 | tf_op jit(solution)/shard_map/while/body/skgqp,spkd->sqkgd/dot_general | solution.py:624
  357.9 9.1 %fusion.193 = bf16[1,512,8,128]{3,1,2,0:T(8,128)(2,1)} fusion(bf16[1,512,8,2,128]{4,1,3,2,0:T(8,128)(2,1)S(1)} %get-tuple-element.806, f32[1,8,2,512,512]{3,4,2,1,0:T(8,128)} %fusion.191), kind=kOutput, calls=%fused_computation.56.clone.1 | convolution fusion | flops 1077936128 | bytes 19922944 | tf_op jit(solution)/shard_map/while/body/skgqp,sqkgd->spkd/dot_general | solution.py:635
  368.5 7.3 fusion.194
  375.8 2.3 copy.105
  378.0 2.8 constant_dynamic-update-slice_fusion.3
  381.8 2.7 bitcast_multiply_fusion.3
  386.7 5.2 multiply_reduce_fusion
  392.0 4.5 convolution_convert_fusion.4
  396.4 5.5 convolution_convert_fusion.1
  401.9 5.4 convolution_convert_fusion
  407.4 4.8 multiply_convert_fusion.1
  412.3 4.7 convolution_convert_fusion.3
  417.0 5.6 convolution_convert_fusion.2
  422.6 4.4 fusion.95
  427.0 66.7 %reduce-scatter.3.cloned.1.call-done = bf16[1,512,1024]{1,2,0:T(8,128)(2,1)} async-done(((bf16[1,1024,1024]{1,2,0:T(8,128)(2,1)}), bf16[1,512,1024]{1,2,0:T(8,128)(2,1)}) %reduce-scatter.3.cloned.1.call-update) | async-done | bytes 1048592 | tf_op jit(solution)/shard_map/reduce_scatter | solution.py:659
  499.1 2.9 convolution_convert_fusion.7
  502.0 2.6 fusion.128
  504.6 23.2 %reduce-scatter.5.cloned.1.call-done = bf16[1,512,1024]{1,2,0:T(8,128)(2,1)} async-done(((bf16[1,1024,1024]{1,2,0:T(8,128)(2,1)}), bf16[1,512,1024]{1,2,0:T(8,128)(2,1)}) %reduce-scatter.5.cloned.1.call-update) | async-done | bytes 1048592 | tf_op jit(solution)/shard_map/reduce_scatter | solution.py:665
  527.8 3.4 fusion.99
  532.2 4.3 fusion.88
  536.5 3.0 convolution_convert_fusion.6
  539.5 208.4 %reduce_grads.1 = (f32[192,1024]{1,0:T(8,128)}, f32[64,3072]{1,0:T(8,128)}, f32[64,3072]{1,0:T(8,128)}, f32[128,1024]{1,0:T(8,128)}, f32[64,2048]{1,0:T(8,128)}, /*index=5*/f32[64,1024]{1,0:T(8,128)}, f32[64,1024]{1,0:T(8,128)}) custom-call(bf16[4,2,2,192,1024]{4,3,2,1,0:T(8,128)(2,1)} %bitcast.401, bf16[4,2,2,64,3072]{4,3,2,1,0:T(8,128)(2,1)} %bitcast.399, ...), custom_call_target="tpu_custom_call" | custom-call | tf_op jit(solution)/shard_map/reduce_grads/pallas_call | solution.py:464
  748.0 3.1 fusion.96
  751.1 43.9 %all-reduce = (f32[1024]{0:T(1024)}, f32[128]{0:T(128)}, f32[128]{0:T(128)}, f32[1024]{0:T(1024)}) all-reduce(f32[1024]{0:T(1024)S(1)} %get-tuple-element.365, f32[128]{0:T(128)S(1)} %get-tuple-element.359, f32[128]{0:T(128)S(1)} %get-tuple-element.361, f32[1024]{0:T(1024)S(1)} %copy-done.47), channel_id=1, replica_groups=mesh['fsdp'=16,'ctx'=2] {'fsdp','ctx'}, use_global_device_ids=true, to_apply=%region_19.20 | all-reduce | flops 2304 | bytes 18432 | tf_op jit(solution)/shard_map/psum | solution.py:690
  795.1 1.9 copy.142
  796.9 1.7 copy.143
  798.7 1.7 copy.144
  (188 shorter events, 31.9 us)
Async XLA Ops:
  7.2 139.8 %copy-start.17 = (bf16[1,512,1024]{2,1,0:T(8,128)(2,1)S(1)}, bf16[1,512,1024]{2,1,0:T(8,128)(2,1)}, u32[]{:S(2)}) copy-start(bf16[1,512,1024]{2,1,0:T(8,128)(2,1)} %param.20) | copy-start | bytes 3145732
  7.2 139.8 %copy-start.45 = (f32[1024]{0:T(1024)S(1)}, f32[1024]{0:T(1024)}, u32[]{:S(2)}) copy-start(f32[1024]{0:T(1024)} %param.23) | copy-start | bytes 12292
  7.2 175.2 %all-gather.6.cloned.1.call-start = ((), (), s32[]{:S(2)}) async-start(), calls=%async_computation.5 | async-start | bytes 3145728 | tf_op jit(solution)/shard_map/all_gather | solution.py:526
  8.8 160.5 %copy-start.39 = (f32[512]{0:T(512)}, f32[512]{0:T(512)S(1)}, u32[]{:S(2)}) copy-start(f32[512]{0:T(512)S(1)} %add_rsqrt_fusion.3) | copy-start | bytes 6148
  150.9 66.8 %all-gather.4.cloned.1.call-start = ((), (), s32[]{:S(2)}) async-start(), calls=%async_computation.2 | async-start | bytes 3145728 | tf_op jit(solution)/shard_map/all_gather | solution.py:525
  150.9 3.9 copy-start.48
  155.9 19.7 %copy-start.6 = (f32[512,128]{0,1:T(8,128)}, f32[512,128]{0,1:T(8,128)S(1)}, u32[]{:S(2)}) copy-start(f32[512,128]{0,1:T(8,128)S(1)} %get-tuple-element.455) | copy-start | bytes 786436
  155.9 19.7 %copy-start.14 = (f32[512,128]{0,1:T(8,128)}, f32[512,128]{0,1:T(8,128)S(1)}, u32[]{:S(2)}) copy-start(f32[512,128]{0,1:T(8,128)S(1)} %get-tuple-element.456) | copy-start | bytes 786436
  156.0 3.4 copy-start.41
  162.4 331.3 %reduce-scatter.3.cloned.1.call-start = ((), (), s32[]{:S(2)}) async-start(), calls=%async_computation.3 | async-start | bytes 3145728 | tf_op jit(solution)/shard_map/reduce_scatter | solution.py:659
  169.3 4.7 copy-start.43
  174.0 2.7 copy-start.2
  174.0 2.6 copy-start.30
  254.4 3.3 copy-start
  254.4 3.3 copy-start.18
  254.4 5.1 copy-start.49
  257.8 4.3 copy-start.21
  257.8 4.6 slice-start.6
  259.6 2.5 copy-start.38
  259.6 2.8 slice-start.7
  259.6 8.2 %slice-start.4 = ((s8[6291456]{0:T(1024)(128)(4,1)}), s8[4194304]{0:T(1024)(128)(4,1)S(1)}, s32[]{:S(2)}) async-start(s8[6291456]{0:T(1024)(128)(4,1)} %bitcast.433), calls=%async_computation.10 | async-start | bytes 8388608
  262.0 33.6 %copy-start.12 = (f32[512,1024]{1,0:T(8,128)}, f32[512,1024]{1,0:T(8,128)S(1)}, u32[]{:S(2)}) copy-start(f32[512,1024]{1,0:T(8,128)S(1)} %get-tuple-element.464) | copy-start | bytes 6291460
  262.1 5.7 slice-start.5
  262.3 5.5 copy-start.26
  262.4 10.9 %slice-start = ((s8[6291456]{0:T(1024)(128)(4,1)}), s8[4194304]{0:T(1024)(128)(4,1)S(1)}, s32[]{:S(2)}) async-start(s8[6291456]{0:T(1024)(128)(4,1)} %bitcast.429), calls=%async_computation.6 | async-start | bytes 8388608
  267.8 5.4 copy-start.28
  267.8 5.4 slice-start.1
  283.7 7.7 copy-start.53
  295.7 2.9 copy-start.50
  306.5 2.3 copy-start.9
  330.4 9.8 %copy-start.1 = (bf16[1,1024,8,128]{3,2,1,0:T(8,128)(2,1)S(1)}, bf16[1,1024,8,128]{3,2,1,0:T(8,128)(2,1)}, u32[]{:S(2)}) copy-start(bf16[1,1024,8,128]{3,2,1,0:T(8,128)(2,1)} %get-tuple-element.805) | copy-start | bytes 6291460 | tf_op jit(solution)/shard_map/while
  380.9 146.9 %reduce-scatter.5.cloned.1.call-start = ((), (), s32[]{:S(2)}) async-start(), calls=%async_computation.4 | async-start | bytes 3145728 | tf_op jit(solution)/shard_map/reduce_scatter | solution.py:665
  384.5 2.2 copy-start.3
  384.5 2.2 copy-start.7
  384.5 2.2 copy-start.31
  384.6 2.2 copy-start.44
  386.7 5.2 copy-start.11
  386.7 5.2 copy-start.22
  391.9 4.5 copy-start.27
  392.0 4.5 copy-start.54
  396.4 5.5 copy-start.55
  407.4 4.8 copy-start.19
  407.4 4.8 copy-start.40
  407.4 4.8 copy-start.46
  412.2 4.7 copy-start.24
  412.3 4.7 copy-start.29
  412.3 4.7 copy-start.56
  412.3 10.3 %slice-start.2 = ((s8[6291456]{0:T(1024)(128)(4,1)}), s8[4194304]{0:T(1024)(128)(4,1)S(1)}, s32[]{:S(2)}) async-start(s8[6291456]{0:T(1024)(128)(4,1)} %bitcast.431), calls=%async_computation.8 | async-start | bytes 8388608
  417.0 5.6 copy-start.13
  417.0 5.6 slice-start.3
  495.2 1.6 copy-start.5
  495.2 1.8 copy-start.8
  495.3 1.8 copy-start.37
  495.3 1.8 copy-start.42
  499.1 2.9 copy-start.23
  527.8 3.4 copy-start.16
  527.8 3.8 copy-start.25
  527.8 4.4 copy-start.52
  532.2 4.3 copy-start.51
  748.0 3.2 copy-start.47
  751.1 49.2 %copy-start.35 = (f32[128,1024]{1,0:T(8,128)S(1)}, f32[128,1024]{1,0:T(8,128)}, u32[]{:S(2)}) copy-start(f32[128,1024]{1,0:T(8,128)} %get-tuple-element.834) | copy-start | bytes 1572868
  751.1 50.0 %copy-start.34 = (f32[64,3072]{1,0:T(8,128)S(1)}, f32[64,3072]{1,0:T(8,128)}, u32[]{:S(2)}) copy-start(f32[64,3072]{1,0:T(8,128)} %get-tuple-element.836) | copy-start | bytes 2359300
  796.9 5.1 copy-start.33
  800.4 2.6 copy-start.32
  (5 other events, 6.2 us)
Sparse Core Ops, SparseCore 0:
  151.0 31.4 all-gather.5
  184.5 33.0 all-gather.3
  381.0 112.6 reduce-scatter.2
  495.9 31.8 reduce-scatter.4
